TPU v7x, 256 devices: a whole 4x4x8 slice. The times are simulated.
256 devices in a mesh: tm: 64 (over z, y, core), pix: 4 (over x).
Axes of the slice: x: 4, y: 4, z: 8, core: 2. Of those that a mesh axis runs over, the one named last changes fastest.
Arguments:
- frames: bfloat16 [1024, 131072], P('tm', 'pix'), may hold values from -30 to 30, as said below
- band_edges: int32 [65], replicated, may hold values from 0 to 384, as said below
Outputs:
- coherence: float32 [64, 2, 8, 8], P('tm')
Inputs may be any that keep to these rules, and one draw needn't show every extreme that they name: `frames`: image intensities with a level of their own in each pixel. Strictly increasing, band_edges[0] = 0 and band_edges[64] = 384; the bands have uneven widths.
All inputs are finite; a program needn't handle non-finite values.
Results may differ from a plain program's by a relative error of at most 0.0096.
Values may be sent and summed in bfloat16 or wider, within the bound.
No kernel may reach another device: no remote copies, remote signals or barrier semaphores. Data moves between devices by JAX's collectives and lax.ppermute only.
A program may use at most 128 MiB of HBM per device.

v0:
```python
import math

import jax
import jax.numpy as jnp
from jax import lax
from jax.sharding import PartitionSpec as P

TAPERS = 8
NB = 384
NBANDS = 64


def partner(value, axis, bit):
    mask = 2**bit
    pairs = [(source, source ^ mask) for source in range(lax.axis_size(axis))]
    return lax.ppermute(value, axis, pairs)


def transform_table(length, bins, tapers):
    frame_ids = jnp.arange(length, dtype=jnp.int32)
    bin_ids = jnp.arange(bins, dtype=jnp.int32)
    phase = (bin_ids[:, None] * frame_ids[None, :] % length).astype(jnp.float32) * (
        2.0 * math.pi / length
    )
    orders = jnp.arange(1, tapers + 1, dtype=jnp.int32).astype(jnp.float32)
    taper_rows = math.sqrt(2.0 / (length + 1)) * jnp.sin(
        math.pi * orders[:, None] * (frame_ids[None, :].astype(jnp.float32) + 1.0) / (length + 1)
    )
    real_part = taper_rows[:, None, :] * jnp.cos(phase)[None]
    imag_part = -taper_rows[:, None, :] * jnp.sin(phase)[None]
    dft_table = jnp.stack([real_part, imag_part], axis=1)
    return dft_table.reshape(tapers * 2 * bins, length).astype(jnp.bfloat16)


def bin_cross(spectra, tapers, bins):
    rows_by_part = spectra.reshape(2 * tapers, bins, -1)
    per_bin = jnp.einsum(
        "afp,bfp->fab", rows_by_part, rows_by_part, precision=lax.Precision.HIGHEST
    )
    return per_bin.reshape(bins, 4 * tapers * tapers)


def band_matrix(band_edges, bins):
    bin_ids = jnp.arange(bins, dtype=jnp.int32)
    band_mask = (bin_ids[None, :] >= band_edges[:-1, None]) & (
        bin_ids[None, :] < band_edges[1:, None]
    )
    return band_mask.astype(jnp.float32)


def coherence_of(band_sums, counts, total_pixels, tapers):
    blocks = band_sums.reshape(-1, tapers, 2, tapers, 2)
    real_part = blocks[:, :, 0, :, 0] + blocks[:, :, 1, :, 1]
    imag_part = blocks[:, :, 1, :, 0] - blocks[:, :, 0, :, 1]
    power_diag = jnp.diagonal(real_part, axis1=1, axis2=2) + 1e-06
    denominator = jnp.sqrt(power_diag[:, :, None] * power_diag[:, None, :])
    scaling = jnp.sqrt(counts * jnp.float32(total_pixels))[:, None, None]
    off_diagonal = 1.0 - jnp.eye(tapers, dtype=jnp.float32)
    factor = scaling * off_diagonal / denominator
    return jnp.stack([real_part * factor, imag_part * factor], axis=1)


def local(frames, band_edges):
    groups = lax.axis_size("tm")
    frames_dev, pix_dev = frames.shape
    share_cols = pix_dev // groups
    frame_total = frames_dev * groups
    dft_table = transform_table(frame_total, NB, TAPERS)
    position = lax.axis_index("tm")
    partner_order = jnp.bitwise_xor(jnp.arange(groups, dtype=jnp.int32), position)
    slot_data = frames.reshape(frames_dev, groups, share_cols).transpose(1, 0, 2)
    slot_data = jnp.take(slot_data, partner_order, axis=0)
    for level in range(groups.bit_length() - 1):
        stride = 1 << level
        halves = slot_data.reshape(groups // (2 * stride), 2, stride, frames_dev, share_cols)
        received = partner(halves[:, 1], "tm", level)
        slot_data = jnp.stack([halves[:, 0], received], axis=1).reshape(
            groups, frames_dev, share_cols
        )
    slot_data = jnp.take(slot_data, partner_order, axis=0)
    widened = slot_data.reshape(frame_total, share_cols).astype(jnp.float32)
    frame_mean = jnp.mean(widened, axis=0, keepdims=True)
    centered = (widened - frame_mean).astype(jnp.bfloat16)
    spectra = jnp.dot(dft_table, centered, preferred_element_type=jnp.float32)
    per_bin = bin_cross(spectra, TAPERS, NB)
    band_mask = band_matrix(band_edges, NB)
    partial_value = jnp.dot(band_mask, per_bin, precision=lax.Precision.HIGHEST)
    counts = jnp.sum(band_mask, axis=1)
    own_bands = NBANDS // groups
    first_band = lax.axis_index("tm") * own_bands
    total_pixels = pix_dev * lax.axis_size("pix")
    summed = lax.psum(partial_value, ("tm", "pix"))
    own_sums = lax.dynamic_slice_in_dim(summed, first_band, own_bands, 0)
    own_counts = lax.dynamic_slice_in_dim(counts, first_band, own_bands, 0)
    return coherence_of(own_sums, own_counts, total_pixels, TAPERS)


def solution(mesh):
    return jax.shard_map(
        local,
        mesh=mesh,
        in_specs=(P("tm", "pix"), P()),
        out_specs=P("tm", None, None, None),
        check_vma=False,
    )
```

profile of v0, /device:TPU:1, one launch (start us, length us, event | category | flops | bytes accessed | tf_op | source)
XLA Modules:
  0.0 409.0 jit_solution(15322427885257564070)
XLA Ops:
  6.6 1.4 copy.32
  7.9 0.6 gather_fusion.1
  8.6 0.2 broadcast_select_fusion
  8.8 3.3 collective-permute-start
  12.1 1.5 collective-permute-done
  13.9 13.1 %collective-permute-done.1 = bf16[16,2,16,512]{3,2,0,1:T(8,128)(2,1)S(1)} collective-permute-done((bf16[16,2,16,512]{3,2,0,1:T(8,128)(2,1)S(1)}, bf16[16,2,16,512]{3,2,0,1:T(8,128)(2,1)S(1)}, u32[]{:S(2)}, u32[]{:S(2)}) %collective-permute-start.1) | collective-permute-done | bytes 524320 | tf_op jit(solution)/shard_map/ppermute | solution.py:16
  27.3 1.3 collective-permute-start.2
  28.6 12.5 %collective-permute-done.2 = bf16[8,4,16,512]{3,2,1,0:T(8,128)(2,1)S(1)} collective-permute-done((bf16[8,4,16,512]{3,2,1,0:T(8,128)(2,1)S(1)}, bf16[8,4,16,512]{3,2,1,0:T(8,128)(2,1)S(1)}, u32[]{:S(2)}, u32[]{:S(2)}) %collective-permute-start.2) | collective-permute-done | bytes 524320 | tf_op jit(solution)/shard_map/ppermute | solution.py:16
  41.3 0.3 collective-permute-start.3
  41.6 5.7 %fusion.7 = f32[384,1024]{1,0:T(8,128)S(1)} fusion(), kind=kLoop, calls=%fused_computation.28 | loop fusion | flops 5505024 | bytes 1572864 | tf_op jit(solution)/shard_map/sin | solution.py:30
  47.3 5.7 %fusion.8 = f32[384,1024]{1,0:T(8,128)S(1)} fusion(), kind=kLoop, calls=%fused_computation.29 | loop fusion | flops 5505024 | bytes 1572864 | tf_op jit(solution)/shard_map/cos | solution.py:29
  52.9 0.4 sine_multiply_fusion
  53.6 3.0 collective-permute-start.4
  56.5 19.0 %multiply_convert_fusion = (bf16[8,1,384,1024]{3,1,0,2:T(2,128)(2,1)S(1)}, bf16[8,1,384,1024]{3,1,0,2:T(2,128)(2,1)}) fusion(f32[384,1024]{1,0:T(8,128)S(1)} %fusion.7, f32[8,1024]{1,0:T(8,128)S(1)} %get-tuple-element.21, f32[384,1024]{1,0:T(8,128)S(1)} %fusion.8, f32[8,1024]{1,0:T(8,128)S(1)} %get-tuple-element.20), kind=kLoop, calls=%fused_computation.4 | loop fusion | flops 12582912 | bytes 15794176 | tf_op jit(solution)/shard_map/convert.1
  75.6 3.9 collective-permute-done.4
  79.6 5.7 %collective-permute-start.5 = (bf16[1,32,16,512]{3,2,1,0:T(8,128)(2,1)S(1)}, bf16[1,32,16,512]{3,2,1,0:T(8,128)(2,1)S(1)}, u32[]{:S(2)}, u32[]{:S(2)}) collective-permute-start(bf16[1,32,16,512]{3,2,1,0:T(8,128)(2,1)S(1)} %get-tuple-element.9), channel_id=1, source_target_pairs={{0,128},{4,132},{8,136},{12,140},{16,144},{20,148},{24,152},{28,15... | collective-permute-start | bytes 1572872 | tf_op jit(solution)/shard_map/ppermute | solution.py:16
  85.3 30.9 %pad_maximum_fusion = bf16[8,2,384,1024]{3,1,0,2:T(2,128)(2,1)} fusion(bf16[8,1,384,1024]{3,1,0,2:T(2,128)(2,1)S(1)} %get-tuple-element.26, bf16[8,1,384,1024]{3,1,0,2:T(2,128)(2,1)} %get-tuple-element.27), kind=kLoop, calls=%fused_computation.3 | loop fusion | flops 25165824 | bytes 25165824 | tf_op jit(solution)/shard_map/stack | solution.py:31
  116.2 19.0 %convert_element_type.75 = bf16[16,384,1024]{2,0,1:T(8,128)(2,1)} reshape(bf16[8,2,384,1024]{3,1,0,2:T(2,128)(2,1)} %pad_maximum_fusion) | data formatting | bytes 25165824 | tf_op jit(solution)/shard_map/convert_element_type | solution.py:32
  135.3 0.7 convert_reduce_fusion.1
  136.1 0.6 gather_fusion.2
  136.8 0.4 convert_reduce_fusion
  137.2 0.3 fusion
  137.5 9.4 %fusion.25 = f32[16,384,512]{2,0,1:T(8,128)S(1)} fusion(bf16[16,384,1024]{2,0,1:T(8,128)(2,1)} %convert_element_type.75, bf16[1024,512,1]{1,0,2:T(8,128)(2,1)S(1)} %bitcast.64), kind=kOutput, calls=%fused_computation.71 | convolution fusion | flops 6442450944 | bytes 26214400 | tf_op jit(solution)/shard_map/dot_general | solution.py:84
  146.9 14.1 %fusion.26 = f32[384,16,16]{2,1,0:T(8,128)S(1)} fusion(f32[16,384,512]{2,0,1:T(8,128)S(1)} %fusion.25), kind=kOutput, calls=%fused_computation.72 | convolution fusion | flops 603979776 | bytes 12976128 | tf_op jit(solution)/shard_map/afp,bfp->fab/dot_general | solution.py:37
  161.0 1.1 copy.26
  162.1 1.0 fusion.12
  163.2 0.6 dynamic_slice.7
  164.5 235.3 %all-reduce.2.cloned.1.call-done = f32[64,256]{1,0:T(8,128)} async-done(((f32[64,256]{1,0:T(8,128)}), f32[64,256]{1,0:T(8,128)}) %all-reduce.2.cloned.1.call-update) | async-done | bytes 65552 | tf_op jit(solution)/shard_map/psum | solution.py:92
  399.7 0.7 dynamic-slice_reduce_fusion
  400.6 0.2 fusion.17
  400.8 0.6 gather_fusion
  401.5 0.6 pad_maximum_fusion.7
  (32 shorter events, 1.5 us)
Async XLA Ops:
  6.5 393.2 %all-reduce.2.cloned.1.call-start = ((), (), s32[]{:S(2)}) async-start(), calls=%async_computation | async-start | bytes 131072 | tf_op jit(solution)/shard_map/psum | solution.py:92
  8.8 4.9 %collective-permute-start = (bf16[32,1,16,512]{3,2,0,1:T(8,128)(2,1)S(1)}, bf16[32,1,16,512]{3,2,0,1:T(8,128)(2,1)S(1)}, u32[]{:S(2)}, u32[]{:S(2)}) collective-permute-start(bf16[32,1,16,512]{3,2,0,1:T(8,128)(2,1)S(1)} %get-tuple-element.19), channel_id=1, source_target_pairs={{0,4},{4,0},{8,12},{12,8},{16,20},{20,16},{24,28},{28,24},{32,36},... | collective-permute-start | bytes 1572872 | tf_op jit(solution)/shard_map/ppermute | solution.py:16
  13.8 13.2 %collective-permute-start.1 = (bf16[16,2,16,512]{3,2,0,1:T(8,128)(2,1)S(1)}, bf16[16,2,16,512]{3,2,0,1:T(8,128)(2,1)S(1)}, u32[]{:S(2)}, u32[]{:S(2)}) collective-permute-start(bf16[16,2,16,512]{3,2,0,1:T(8,128)(2,1)S(1)} %get-tuple-element.17), channel_id=1, source_target_pairs={{0,8},{4,12},{8,0},{12,4},{16,24},{20,28},{24,16},{28,20},{32,40},... | collective-permute-start | bytes 1572872 | tf_op jit(solution)/shard_map/ppermute | solution.py:16
  27.3 13.8 %collective-permute-start.2 = (bf16[8,4,16,512]{3,2,1,0:T(8,128)(2,1)S(1)}, bf16[8,4,16,512]{3,2,1,0:T(8,128)(2,1)S(1)}, u32[]{:S(2)}, u32[]{:S(2)}) collective-permute-start(bf16[8,4,16,512]{3,2,1,0:T(8,128)(2,1)S(1)} %get-tuple-element.15), channel_id=1, source_target_pairs={{0,16},{4,20},{8,24},{12,28},{16,0},{20,4},{24,8},{28,12},{32,48},... | collective-permute-start | bytes 1572872 | tf_op jit(solution)/shard_map/ppermute | solution.py:16
  41.3 12.1 %collective-permute-start.3 = (bf16[4,8,16,512]{3,2,1,0:T(8,128)(2,1)S(1)}, bf16[4,8,16,512]{3,2,1,0:T(8,128)(2,1)S(1)}, u32[]{:S(2)}, u32[]{:S(2)}) collective-permute-start(bf16[4,8,16,512]{3,2,1,0:T(8,128)(2,1)S(1)} %get-tuple-element.13), channel_id=1, source_target_pairs={{0,32},{4,36},{8,40},{12,44},{16,48},{20,52},{24,56},{28,60},{32,0... | collective-permute-start | bytes 1572872 | tf_op jit(solution)/shard_map/ppermute | solution.py:16
  53.6 25.9 %collective-permute-start.4 = (bf16[2,16,16,512]{3,2,1,0:T(8,128)(2,1)S(1)}, bf16[2,16,16,512]{3,2,1,0:T(8,128)(2,1)S(1)}, u32[]{:S(2)}, u32[]{:S(2)}) collective-permute-start(bf16[2,16,16,512]{3,2,1,0:T(8,128)(2,1)S(1)} %get-tuple-element.11), channel_id=1, source_target_pairs={{0,64},{4,68},{8,72},{12,76},{16,80},{20,84},{24,88},{28,92},{32,9... | collective-permute-start | bytes 1572872 | tf_op jit(solution)/shard_map/ppermute | solution.py:16
  79.6 56.4 %collective-permute-start.5 = (bf16[1,32,16,512]{3,2,1,0:T(8,128)(2,1)S(1)}, bf16[1,32,16,512]{3,2,1,0:T(8,128)(2,1)S(1)}, u32[]{:S(2)}, u32[]{:S(2)}) collective-permute-start(bf16[1,32,16,512]{3,2,1,0:T(8,128)(2,1)S(1)} %get-tuple-element.9), channel_id=1, source_target_pairs={{0,128},{4,132},{8,136},{12,140},{16,144},{20,148},{24,152},{28,15... | collective-permute-start | bytes 1572872 | tf_op jit(solution)/shard_map/ppermute | solution.py:16
  116.2 19.0 %copy-start = (s32[65]{0:T(128)S(1)}, s32[65]{0:T(128)}, u32[]{:S(2)}) copy-start(s32[65]{0:T(128)} %param.5) | copy-start | bytes 784
  161.0 2.2 copy-start.1
Sparse Core Ops, SparseCore 0:
  163.3 236.4 all-reduce.1
where the time goes:
time: 410 us; the launch traced here: 409 us
  waiting for transfers between devices  266 us (65%)
  other arithmetic  64.8 us (16%)
  local copies, waits for them, and re-layouts  25.4 us (6%)
  matrix products  24.5 us (6%)
  between operations  14.3 us (3%)
  starting transfers between devices  13.6 us (3%)
    psum x1, waiting for transfers between devices, local(): summed = lax.psum(partial_value, ('tm', 'pix'))  235 us
    ppermute x6, waiting for transfers between devices, partner(): return lax.ppermute(value, axis, pairs)  31.1 us
    another operation x1, other arithmetic, transform_table(): dft_table = jnp.stack([real_part, imag_part], axis=1)  30.9 us
    convert_element_type x1, local copies, waits for them, and re-layouts, transform_table(): return dft_table.reshape(tapers * 2 * bins, length).astype(jnp.bfloat16)  19 us
    another operation x1, other arithmetic  19 us
    dot_general x1, matrix products, bin_cross(): jnp.einsum('afp,bfp->fab', rows_by_part, rows_by_part, precision=lax.Prec...  14.1 us
    ppermute x6, starting transfers between devices, partner(): return lax.ppermute(value, axis, pairs)  13.6 us
    dot_general x1, matrix products, local(): spectra = jnp.dot(dft_table, centered, preferred_element_type=jnp.float32)  9.45 us
  transfers between devices with their start and end apart: 7, of which 5 were waited for; matrix products, arithmetic and copies ran while one was open for 20% of the time, Pallas kernels for 0%

commit v1 on v0

v1 whole, which is shorter than its diff:
```python
import functools
import math

import jax
import jax.numpy as jnp
from jax import lax
from jax.experimental import pallas as pl
from jax.experimental.pallas import tpu as pltpu
from jax.sharding import PartitionSpec as P

TAPERS = 8
NB = 384
NBANDS = 64
NT = 1024
CHUNK = 16
ROWS = CHUNK * TAPERS
LANES = 128
STEPS = NB // CHUNK
PIECE = 4
SLOTS = 2


FINE_COS, FINE_SIN, COARSE_COS, COARSE_SIN, TAPER = 0, CHUNK, 2 * CHUNK, 2 * CHUNK + STEPS, 2 * (CHUNK + STEPS)
WAVES = TAPER + TAPERS


def wave_kernel(waves_ref):
    def waves(count, stride):
        frame = lax.broadcasted_iota(jnp.int32, (count, NT), 1)
        bins = lax.broadcasted_iota(jnp.int32, (count, NT), 0) * stride
        phase = jnp.bitwise_and(bins * frame, NT - 1).astype(jnp.float32) * (2.0 * math.pi / NT)
        return jnp.cos(phase), jnp.sin(phase)

    cosine, sine = waves(CHUNK, 1)
    waves_ref[pl.ds(FINE_COS, CHUNK), :] = cosine
    waves_ref[pl.ds(FINE_SIN, CHUNK), :] = sine
    cosine, sine = waves(STEPS, CHUNK)
    waves_ref[pl.ds(COARSE_COS, STEPS), :] = cosine
    waves_ref[pl.ds(COARSE_SIN, STEPS), :] = sine
    order = lax.broadcasted_iota(jnp.int32, (TAPERS, NT), 0) + 1
    frame = lax.broadcasted_iota(jnp.int32, (TAPERS, NT), 1) + 1
    angle = (order * frame).astype(jnp.float32) * (math.pi / (NT + 1))
    waves_ref[pl.ds(TAPER, TAPERS), :] = math.sqrt(2.0 / (NT + 1)) * jnp.sin(angle)


def base_waves():
    return pl.pallas_call(
        wave_kernel,
        out_shape=jax.ShapeDtypeStruct((WAVES, NT), jnp.float32),
        cost_estimate=pl.CostEstimate(flops=10_000_000, bytes_accessed=400_000, transcendentals=100_000),
        name="base_waves",
    )()


def spectra_kernel(
    band_ref, keep_ref, waves_ref, data_ref, out_ref, table_ref, wave_ref, centered_ref, spectra_ref, band_sum_ref
):
    pixels = data_ref.shape[1]
    piece_rows = PIECE * 2 * ROWS
    pieces = STEPS // PIECE

    def table(p):
        taper = waves_ref[pl.ds(TAPER, TAPERS), :]
        for j in range(PIECE):
            a = p * PIECE + j
            ca, sa = waves_ref[pl.ds(COARSE_COS + a, 1), :], waves_ref[pl.ds(COARSE_SIN + a, 1), :]
            cb, sb = waves_ref[pl.ds(FINE_COS, CHUNK), :], waves_ref[pl.ds(FINE_SIN, CHUNK), :]
            wave_ref[a % 2, 0] = ca * cb - sa * sb
            wave_ref[a % 2, 1] = -(sa * cb + ca * sb)
            for part in range(2):
                for i in range(0, CHUNK, 2):
                    two = [taper * wave_ref[a % 2, part, pl.ds(i + h, 1), :] for h in range(2)]
                    at = j * 2 * ROWS + part * ROWS + i * TAPERS
                    table_ref[p % SLOTS, pl.ds(at, 2 * TAPERS), :] = jnp.concatenate(two, axis=0).astype(jnp.bfloat16)

    table(0)
    total = jnp.zeros((1, pixels), jnp.float32)
    for g in range(4):
        part = data_ref[pl.ds(g * 256, 256), :].astype(jnp.float32)
        total = total + jnp.sum(part, axis=0, keepdims=True)
    mean = total * (1.0 / NT)
    for g in range(4):
        part = data_ref[pl.ds(g * 256, 256), :].astype(jnp.float32)
        centered_ref[pl.ds(g * 256, 256), :] = (part - mean).astype(jnp.bfloat16)

    lane = lax.broadcasted_iota(jnp.int32, (TAPERS, LANES), 1)
    row = lax.broadcasted_iota(jnp.int32, (TAPERS, LANES), 0)
    is_real = lane < TAPERS

    def transform(p):
        spectra_ref[p % SLOTS] = jnp.dot(
            table_ref[p % SLOTS], centered_ref[...], preferred_element_type=jnp.float32
        ).astype(jnp.bfloat16)

    def cross(p, acc):
        for j in range(PIECE):
            both = spectra_ref[p % SLOTS, pl.ds(j * 2 * ROWS, 2 * ROWS), :]
            gram = lax.dot_general(both, both, (((1,), (1,)), ((), ())), preferred_element_type=jnp.float32)
            for i in range(CHUNK):
                f = (p * PIECE + j) * CHUNK + i
                top, low = i * TAPERS, ROWS + i * TAPERS
                real = gram[top : top + TAPERS, :LANES] + gram[low : low + TAPERS, LANES:]
                imag = gram[low : low + TAPERS, :LANES] - gram[top : top + TAPERS, LANES:]
                real = pltpu.roll(real, (LANES - top) % LANES, 1)
                imag = pltpu.roll(imag, (LANES - top + TAPERS) % LANES, 1)
                acc = acc * keep_ref[f] + jnp.where(is_real, real, imag)
                band_sum_ref[band_ref[f]] = acc
        return acc

    acc = jnp.zeros((TAPERS, LANES), jnp.float32)
    for p in range(pieces):
        transform(p)
        if p + 1 < pieces:
            table(p + 1)
        if p:
            acc = cross(p - 1, acc)
    acc = cross(pieces - 1, acc)
    value = jnp.where((lane < 2 * TAPERS)[None], band_sum_ref[...], 0.0)
    for shift in (16, 32, 64):
        value = value + pltpu.roll(value, shift, 2)
    own = (jnp.right_shift(lane, 4) == row)[None]
    sums = jnp.sum(jnp.where(own, value, 0.0), axis=1, keepdims=True)
    out_ref[...] = jnp.broadcast_to(sums, out_ref.shape)


def band_sums_of(data, waves, band_of, keep, copies):
    pixels = data.shape[1]
    vmem, smem = pl.BlockSpec(memory_space=pltpu.VMEM), pl.BlockSpec(memory_space=pltpu.SMEM)
    macs = 2 * NB * TAPERS * NT * pixels + STEPS * (2 * ROWS) ** 2 * pixels
    return pl.pallas_call(
        spectra_kernel,
        out_shape=jax.ShapeDtypeStruct((NBANDS, copies, LANES), jnp.float32),
        in_specs=[smem, smem, vmem, vmem],
        out_specs=vmem,
        scratch_shapes=[
            pltpu.VMEM((SLOTS, PIECE * 2 * ROWS, NT), jnp.bfloat16),
            pltpu.VMEM((2, 2, CHUNK, NT), jnp.float32),
            pltpu.VMEM((NT, pixels), jnp.bfloat16),
            pltpu.VMEM((SLOTS, PIECE * 2 * ROWS, pixels), jnp.bfloat16),
            pltpu.VMEM((NBANDS, TAPERS, LANES), jnp.float32),
        ],
        cost_estimate=pl.CostEstimate(flops=2 * macs, bytes_accessed=2_000_000, transcendentals=0),
        compiler_params=pltpu.CompilerParams(vmem_limit_bytes=20 * 2**20),
        name="band_sums",
    )(band_of, keep, waves, data)


def coherence_kernel(total_pixels, edges_ref, parts_ref, out_ref):
    own = lax.axis_index("tm")
    count = jnp.full((TAPERS, LANES), edges_ref[own + 1] - edges_ref[own], jnp.int32).astype(jnp.float32)
    scale = jnp.sqrt(count * jnp.float32(total_pixels))
    total = jnp.sum(parts_ref[...], axis=0, keepdims=True)
    lane = lax.broadcasted_iota(jnp.int32, (TAPERS, LANES), 1)
    row = lax.broadcasted_iota(jnp.int32, (TAPERS, LANES), 0)
    value = jnp.where(jnp.right_shift(lane, 4) == row, jnp.broadcast_to(total, (TAPERS, LANES)), 0.0)
    for shift in (16, 32, 64):
        value = value + pltpu.roll(value, shift, 1)
    diag = jnp.where(jnp.bitwise_and(lane, TAPERS * 2 - 1) == row, value, 0.0)
    diag = jnp.where(lane < TAPERS, diag, 0.0)
    power_row = jnp.sum(diag, axis=1, keepdims=True) + 1e-06
    power_lane = jnp.sum(diag, axis=0, keepdims=True)
    power_lane = jnp.where(lane < TAPERS, power_lane, pltpu.roll(jnp.broadcast_to(power_lane, (TAPERS, LANES)), TAPERS, 1)) + 1e-06
    denominator = jnp.sqrt(power_row * power_lane)
    off = jnp.bitwise_and(lane, TAPERS - 1) != row
    result = jnp.where(off, value * scale / denominator, 0.0)
    out_ref[0, 0] = result[:, :TAPERS]
    out_ref[0, 1] = result[:, TAPERS : 2 * TAPERS]


def coherence_of(band_edges, parts, total_pixels):
    return pl.pallas_call(
        functools.partial(coherence_kernel, total_pixels),
        out_shape=jax.ShapeDtypeStruct((1, 2, TAPERS, TAPERS), jnp.float32),
        in_specs=[pl.BlockSpec(memory_space=pltpu.SMEM), pl.BlockSpec(memory_space=pltpu.VMEM)],
        name="coherence",
    )(band_edges, parts)


def local(frames, band_edges):
    groups = lax.axis_size("tm")
    n_pix = lax.axis_size("pix")
    frames_dev, pix_dev = frames.shape
    share = pix_dev // groups
    blocks = frames.reshape(frames_dev, groups, share).transpose(1, 0, 2)
    data = lax.all_to_all(blocks, "tm", 0, 0, tiled=True).reshape(NT, share)
    waves = base_waves()
    bin_ids = jnp.arange(NB, dtype=jnp.int32)
    band_of = jnp.sum((bin_ids[:, None] >= band_edges[None, 1:]).astype(jnp.int32), axis=1)
    keep = 1.0 - jnp.any(bin_ids[:, None] == band_edges[None, :-1], axis=1).astype(jnp.float32)
    sums = band_sums_of(data, waves, band_of, keep, n_pix)
    parts = lax.all_to_all(sums.reshape(groups * n_pix, 1, LANES), ("tm", "pix"), 0, 0, tiled=True)
    return coherence_of(band_edges, parts.reshape(groups * n_pix, LANES), pix_dev * n_pix)


def solution(mesh):
    return jax.shard_map(
        local,
        mesh=mesh,
        in_specs=(P("tm", "pix"), P()),
        out_specs=P("tm", None, None, None),
        check_vma=False,
    )
```

time: 410 us -> 78 us (0.19)
  waiting for transfers between devices: 266 us -> 26.2 us
  other arithmetic: 64.8 us -> 0.2 us
  matrix products: 24.5 us -> 0 us
  local copies, waits for them, and re-layouts: 25.4 us -> 3.43 us
  blocking collectives: 0 us -> 21.6 us
  between operations: 14.3 us -> 0.04 us
  Pallas kernels: 0 us -> 13.1 us
    psum x1 -> x0, waiting for transfers between devices: 235 us -> none  [local(): summed = lax.psum(partial_value, ('tm', 'pix'))]
    another operation x9 -> x0, other arithmetic: 51.2 us -> none  [the longest x1 30.9 us: transform_table(): dft_table = jnp.stack([real_part, imag_part], axis=1)]
    ppermute x6 -> x0, waiting for transfers between devices: 31.1 us -> none  [partner(): return lax.ppermute(value, axis, pairs)]
    all_to_all x0 -> x1, waiting for transfers between devices: none -> 26.2 us  [local(): data = lax.all_to_all(blocks, 'tm', 0, 0, tiled=True).reshape(NT, share)]
    dot_general x3 -> x0, matrix products: 24.5 us -> none  [the longest x1 14.1 us: bin_cross(): jnp.einsum('afp,bfp->fab', rows_by_part, rows_by_part, precision=lax.Prec...]
    all_to_all x0 -> x1, blocking collectives: none -> 21.6 us  [local(): lax.all_to_all(sums.reshape(groups * n_pix, 1, LANES), ('tm', 'pix'), 0,...]
    convert_element_type x1 -> x0, local copies, waits for them, and re-layouts: 19 us -> none  [transform_table(): return dft_table.reshape(tapers * 2 * bins, length).astype(jnp.bfloat16)]
    ppermute x6 -> x0, starting transfers between devices: 13.6 us -> none  [partner(): return lax.ppermute(value, axis, pairs)]
  transfers between devices with their start and end apart: 7 -> 1, of which waited for: 5 -> 1; matrix products, arithmetic and copies ran while one was open for 20% -> 0% of each run, Pallas kernels for 0% -> 2%
where the time goes in v1:
time: 78 us; the launch traced here: 77.7 us
  waiting for transfers between devices  26.2 us (34%)
  blocking collectives  21.6 us (28%)
  starting transfers between devices  13.2 us (17%)
  Pallas kernels  13.1 us (17%)
  local copies, waits for them, and re-layouts  3.43 us (4%)
    all_to_all x1, waiting for transfers between devices, local(): data = lax.all_to_all(blocks, 'tm', 0, 0, tiled=True).reshape(NT, share)  26.2 us
    all_to_all x1, blocking collectives, local(): lax.all_to_all(sums.reshape(groups * n_pix, 1, LANES), ('tm', 'pix'), 0,...  21.6 us
    all_to_all x1, starting transfers between devices, local(): data = lax.all_to_all(blocks, 'tm', 0, 0, tiled=True).reshape(NT, share)  13.2 us
    pallas_call x1, Pallas kernels, band_sums_of(): pl.pallas_call(spectra_kernel, out_shape=jax.ShapeDtypeStruct((NBANDS, co...  9.69 us
    reshape x1, local copies, waits for them, and re-layouts, local(): blocks = frames.reshape(frames_dev, groups, share).transpose(1, 0, 2)  2.37 us
    pallas_call x1, Pallas kernels, coherence_of(): pl.pallas_call(functools.partial(coherence_kernel, total_pixels), out_sha...  1.92 us
  transfers between devices with their start and end apart: 1, of which 1 were waited for; matrix products, arithmetic and copies ran while one was open for 0% of the time, Pallas kernels for 2%

profile of v1, /device:TPU:1, one launch (start us, length us, event | category | flops | bytes accessed | tf_op | source)
XLA Modules:
  0.0 77.7 jit_solution(4815317784569910291)
XLA Ops:
  0.0 2.4 %copy.10 = bf16[2,64,8,512]{3,2,0,1:T(8,128)(2,1)} copy(bf16[2,64,8,512]{3,2,1,0:T(8,128)(2,1)} %bitcast.14) | data formatting | bytes 2097152 | tf_op jit(solution)/shard_map/reshape | solution.py:184
  2.4 13.2 %all-to-all-start = ((bf16[64,16,512]{2,1,0:T(8,128)(2,1)}), bf16[64,16,512]{2,1,0:T(8,128)(2,1)S(1)}, u32[]{:S(2)}, u32[]{:S(2)}) async-start(bf16[64,16,512]{2,1,0:T(8,128)(2,1)} %bitcast.11), calls=%async_computation | async-start | bytes 2097152 | tf_op jit(solution)/shard_map/all_to_all | solution.py:185
  15.5 0.0 copy-start.1
  15.5 1.5 %base_waves.1.waves_ref = f32[88,1024]{1,0:T(8,128)} custom-call(), custom_call_target="tpu_custom_call" | custom-call | flops 10000000 | bytes 400000 | tf_op jit(solution)/shard_map/base_waves/pallas_call | solution.py:47
  17.0 0.0 copy-done.1
  17.0 0.1 fusion.1
  17.1 0.1 fusion
  17.2 0.1 convert_reduce_fusion.band_ref
  17.3 26.2 %all-to-all-done = bf16[64,16,512]{2,1,0:T(8,128)(2,1)S(1)} async-done(((bf16[64,16,512]{2,1,0:T(8,128)(2,1)}), bf16[64,16,512]{2,1,0:T(8,128)(2,1)S(1)}, u32[]{:S(2)}, u32[]{:S(2)}) %all-to-all-start) | async-done | bytes 1048608 | tf_op jit(solution)/shard_map/all_to_all | solution.py:185
  43.5 0.0 copy-start
  43.5 1.0 %copy-done = f32[88,1024]{1,0:T(8,128)S(1)} copy-done((f32[88,1024]{1,0:T(8,128)S(1)}, f32[88,1024]{1,0:T(8,128)}, u32[]{:S(2)}) %copy-start) | copy-done | bytes 360472
  44.5 9.7 %band_sums.1 = f32[64,4,128]{2,1,0:T(4,128)S(1)} custom-call(s32[384]{0:T(512)S(1)} %convert_reduce_fusion.band_ref, f32[384]{0:T(512)S(1)} %convert_subtract_fusion.keep_ref, f32[88,1024]{1,0:T(8,128)S(1)} %copy-done, bf16[1024,512]{1,0:T(8,128)(2,1)S(1)} %bitcast.12), custom_call_target="tpu_custom_call" | custom-call | flops 8053063680 | bytes 2000000 | tf_op jit(solution)/shard_map/band_sums/pallas_call | solution.py:130
  54.2 21.6 %all_to_all.10 = f32[256,1,128]{2,1,0:T(1,128)} all-to-all(f32[256,1,128]{2,1,0:T(1,128)S(1)} %bitcast.13), channel_id=1, replica_groups=mesh['tm'=64,'pix'=4] {'tm','pix'}, dimensions={0} | all-to-all | bytes 262144 | tf_op jit(solution)/shard_map/all_to_all | solution.py:191
  75.8 1.9 %coherence.1 = f32[1,2,8,8]{3,2,1,0:T(8,128)} custom-call(s32[65]{0:T(128)} %edges_ref.1, f32[256,128]{1,0:T(8,128)} %bitcast.15), custom_call_target="tpu_custom_call" | custom-call | tf_op jit(solution)/shard_map/coherence/pallas_call | solution.py:171
  (1 shorter events, 0.0 us)
Async XLA Ops:
  2.4 41.1 %all-to-all-start = ((bf16[64,16,512]{2,1,0:T(8,128)(2,1)}), bf16[64,16,512]{2,1,0:T(8,128)(2,1)S(1)}, u32[]{:S(2)}, u32[]{:S(2)}) async-start(bf16[64,16,512]{2,1,0:T(8,128)(2,1)} %bitcast.11), calls=%async_computation | async-start | bytes 2097152 | tf_op jit(solution)/shard_map/all_to_all | solution.py:185
  15.5 1.5 %copy-start.1 = (s32[65]{0:T(128)S(1)}, s32[65]{0:T(128)}, u32[]{:S(2)}) copy-start(s32[65]{0:T(128)} %edges_ref.1) | copy-start | bytes 784
  43.5 1.0 %copy-start = (f32[88,1024]{1,0:T(8,128)S(1)}, f32[88,1024]{1,0:T(8,128)}, u32[]{:S(2)}) copy-start(f32[88,1024]{1,0:T(8,128)} %base_waves.1.waves_ref) | copy-start | bytes 1081348

commit v2 on v1

v2 whole, which is shorter than its diff:
```python
import functools
import math

import jax
import jax.numpy as jnp
from jax import lax
from jax.experimental import pallas as pl
from jax.experimental.pallas import tpu as pltpu
from jax.sharding import PartitionSpec as P

TAPERS = 8
NB = 384
NBANDS = 64
NT = 1024
CHUNK = 16
ROWS = CHUNK * TAPERS
LANES = 128
STEPS = NB // CHUNK
HALF = NT // 2
SLOTS = 2
MIDDLE = NT // 4
FULL = ((0, 1, 2, 3), (4, 5, 6, 7))
PAIRED = ((8, 9), (10, 11), (12, 13), (14, 15))
PIECES = FULL + PAIRED
PIECE_ROWS = 8 * ROWS


def base_waves():
    column = jnp.arange(NT, dtype=jnp.int32)
    frame = jnp.where(column < HALF, 2 * column, 2 * (column - HALF) + 1)[None]

    def waves(count, stride):
        bins = (jnp.arange(count, dtype=jnp.int32) * stride)[:, None]
        phase = jnp.bitwise_and(bins * frame, NT - 1).astype(jnp.float32) * (2.0 * math.pi / NT)
        return jnp.cos(phase), jnp.sin(phase)

    order = jnp.arange(1, TAPERS + 1, dtype=jnp.int32)[:, None]
    angle = (order * (frame + 1)).astype(jnp.float32) * (math.pi / (NT + 1))
    return *waves(CHUNK, 1), *waves(STEPS, CHUNK), math.sqrt(2.0 / (NT + 1)) * jnp.sin(angle)


def spectra_kernel(
    band_ref, keep_ref, fine_cos, fine_sin, coarse_cos, coarse_sin, taper_ref, data_ref, out_ref,
    wide_ref, table_ref, wave_ref, centered_ref, spectra_ref, middle_ref, low_sum_ref, high_sum_ref,
):
    pixels = data_ref.shape[1]

    def wave(a, slot):
        ca, sa = coarse_cos[pl.ds(a, 1), :], coarse_sin[pl.ds(a, 1), :]
        cb, sb = fine_cos[...], fine_sin[...]
        wave_ref[slot, 0] = ca * cb - sa * sb
        wave_ref[slot, 1] = -(sa * cb + ca * sb)

    def table(p):
        taper = taper_ref[...]
        for j, a in enumerate(PIECES[p]):
            wave(a, a % 2)
            for part in range(2):
                for i in range(0, CHUNK, 2):
                    two = [taper * wave_ref[a % 2, part, pl.ds(i + h, 1), :] for h in range(2)]
                    at = j * 2 * ROWS + part * ROWS + i * TAPERS
                    table_ref[p % SLOTS, pl.ds(at, 2 * TAPERS), :] = jnp.concatenate(two, axis=0).astype(jnp.bfloat16)
        if p == len(FULL) - 1:
            wave(MIDDLE // CHUNK, 2)
            two = [taper * wave_ref[2, part, pl.ds(0, 1), :] for part in range(2)]
            table_ref[p % SLOTS, pl.ds(PIECE_ROWS, 2 * TAPERS), :] = jnp.concatenate(two, axis=0).astype(jnp.bfloat16)

    table(0)
    low_sum_ref[...] = jnp.zeros(low_sum_ref.shape, jnp.float32)
    high_sum_ref[...] = jnp.zeros(high_sum_ref.shape, jnp.float32)
    total = jnp.zeros((1, pixels), jnp.float32)
    for g in range(4):
        part = data_ref[pl.ds(g * 256, 256), :].astype(jnp.float32)
        total = total + jnp.sum(part, axis=0, keepdims=True)
        for h in range(pixels // LANES):
            wide_ref[h, pl.ds(g * 256, 256), :] = part[:, h * LANES : (h + 1) * LANES]
    mean = total * (1.0 / NT)
    for odd in range(2):
        for h in range(pixels // LANES):
            part = wide_ref[h, pl.ds(odd, HALF, stride=2), :] - mean[:, h * LANES : (h + 1) * LANES]
            centered_ref[pl.ds(odd * HALF, HALF), h * LANES : (h + 1) * LANES] = part.astype(jnp.bfloat16)

    lane = lax.broadcasted_iota(jnp.int32, (TAPERS, LANES), 1)
    row = lax.broadcasted_iota(jnp.int32, (TAPERS, LANES), 0)
    is_real = lane < TAPERS

    def transform(p):
        slot = p % SLOTS
        if p < len(FULL):
            rows = PIECE_ROWS + (2 * TAPERS if p == len(FULL) - 1 else 0)
            value = jnp.dot(table_ref[slot, pl.ds(0, rows), :], centered_ref[...], preferred_element_type=jnp.float32)
            spectra_ref[slot] = value[:PIECE_ROWS].astype(jnp.bfloat16)
            if rows > PIECE_ROWS:
                middle_ref[...] = value[PIECE_ROWS:]
            return
        rows = PIECE_ROWS // 2
        even = jnp.dot(
            table_ref[slot, pl.ds(0, rows), pl.ds(0, HALF)], centered_ref[pl.ds(0, HALF), :], preferred_element_type=jnp.float32
        )
        odd = jnp.dot(
            table_ref[slot, pl.ds(0, rows), pl.ds(HALF, HALF)], centered_ref[pl.ds(HALF, HALF), :], preferred_element_type=jnp.float32
        )
        spectra_ref[slot, pl.ds(0, rows), :] = (even + odd).astype(jnp.bfloat16)
        mirror = even - odd
        if p == len(FULL):
            mirror = jnp.concatenate(
                [
                    middle_ref[pl.ds(0, TAPERS), :],
                    mirror[TAPERS:ROWS],
                    -middle_ref[pl.ds(TAPERS, TAPERS), :],
                    mirror[ROWS + TAPERS :],
                ],
                axis=0,
            )
        spectra_ref[slot, pl.ds(rows, rows), :] = mirror.astype(jnp.bfloat16)

    def values(p, j, mirrored):
        both = spectra_ref[p % SLOTS, pl.ds(j * 2 * ROWS, 2 * ROWS), :]
        gram = lax.dot_general(both, both, (((1,), (1,)), ((), ())), preferred_element_type=jnp.float32)
        found = []
        for i in range(CHUNK):
            top, low = i * TAPERS, ROWS + i * TAPERS
            real = gram[top : top + TAPERS, :LANES] + gram[low : low + TAPERS, LANES:]
            imag = gram[low : low + TAPERS, :LANES] - gram[top : top + TAPERS, LANES:]
            if mirrored:
                imag = -imag
            real = pltpu.roll(real, (LANES - top) % LANES, 1)
            imag = pltpu.roll(imag, (LANES - top + TAPERS) % LANES, 1)
            found.append(jnp.where(is_real, real, imag))
        return found

    zero = jnp.zeros((TAPERS, LANES), jnp.float32)
    state = {"low": zero, "high": zero, "middle": zero}

    def add_high(f, value):
        state["high"] = state["high"] * keep_ref[f + 1] + value
        high_sum_ref[band_ref[f]] = state["high"]

    def cross(p):
        for j, a in enumerate(PIECES[p]):
            for i, value in enumerate(values(p, j, False)):
                f = a * CHUNK + i
                state["low"] = state["low"] * keep_ref[f] + value
                low_sum_ref[band_ref[f]] = state["low"]
        if p < len(FULL):
            return
        for j, a in enumerate(PIECES[p]):
            for i, value in enumerate(values(p, len(PIECES[p]) + j, True)):
                f = HALF - (a * CHUNK + i)
                if f == NB:
                    state["middle"] = value
                else:
                    add_high(f, value)

    for p in range(len(PIECES)):
        transform(p)
        if p + 1 < len(PIECES):
            table(p + 1)
        if p:
            cross(p - 1)
    cross(len(PIECES) - 1)
    add_high(MIDDLE, state["middle"])
    value = jnp.where((lane < 2 * TAPERS)[None], low_sum_ref[...] + high_sum_ref[...], 0.0)
    for shift in (16, 32, 64):
        value = value + pltpu.roll(value, shift, 2)
    own = (jnp.right_shift(lane, 4) == row)[None]
    sums = jnp.sum(jnp.where(own, value, 0.0), axis=1, keepdims=True)
    out_ref[...] = jnp.broadcast_to(sums, out_ref.shape)


def band_sums_of(data, waves, band_of, keep, copies):
    pixels = data.shape[1]
    vmem, smem = pl.BlockSpec(memory_space=pltpu.VMEM), pl.BlockSpec(memory_space=pltpu.SMEM)
    macs = NB * TAPERS * NT * pixels * 4 // 3 + STEPS * (2 * ROWS) ** 2 * pixels
    return pl.pallas_call(
        spectra_kernel,
        out_shape=jax.ShapeDtypeStruct((NBANDS, copies, LANES), jnp.float32),
        in_specs=[smem, smem] + [vmem] * 6,
        out_specs=vmem,
        scratch_shapes=[
            pltpu.VMEM((pixels // LANES, NT, LANES), jnp.float32),
            pltpu.VMEM((SLOTS, PIECE_ROWS + 2 * TAPERS, NT), jnp.bfloat16),
            pltpu.VMEM((3, 2, CHUNK, NT), jnp.float32),
            pltpu.VMEM((NT, pixels), jnp.bfloat16),
            pltpu.VMEM((SLOTS, PIECE_ROWS, pixels), jnp.bfloat16),
            pltpu.VMEM((2 * TAPERS, pixels), jnp.float32),
            pltpu.VMEM((NBANDS, TAPERS, LANES), jnp.float32),
            pltpu.VMEM((NBANDS, TAPERS, LANES), jnp.float32),
        ],
        cost_estimate=pl.CostEstimate(flops=2 * macs, bytes_accessed=2_000_000, transcendentals=0),
        compiler_params=pltpu.CompilerParams(vmem_limit_bytes=28 * 2**20),
        name="band_sums",
    )(band_of, keep, *waves, data)


def coherence_kernel(total_pixels, edges_ref, parts_ref, out_ref):
    own = lax.axis_index("tm")
    count = jnp.full((TAPERS, LANES), edges_ref[own + 1] - edges_ref[own], jnp.int32).astype(jnp.float32)
    scale = jnp.sqrt(count * jnp.float32(total_pixels))
    total = jnp.sum(parts_ref[...], axis=0, keepdims=True)
    lane = lax.broadcasted_iota(jnp.int32, (TAPERS, LANES), 1)
    row = lax.broadcasted_iota(jnp.int32, (TAPERS, LANES), 0)
    value = jnp.where(jnp.right_shift(lane, 4) == row, jnp.broadcast_to(total, (TAPERS, LANES)), 0.0)
    for shift in (16, 32, 64):
        value = value + pltpu.roll(value, shift, 1)
    diag = jnp.where(jnp.bitwise_and(lane, TAPERS * 2 - 1) == row, value, 0.0)
    diag = jnp.where(lane < TAPERS, diag, 0.0)
    power_row = jnp.sum(diag, axis=1, keepdims=True) + 1e-06
    power_lane = jnp.sum(diag, axis=0, keepdims=True)
    power_lane = jnp.where(lane < TAPERS, power_lane, pltpu.roll(jnp.broadcast_to(power_lane, (TAPERS, LANES)), TAPERS, 1)) + 1e-06
    denominator = jnp.sqrt(power_row * power_lane)
    off = jnp.bitwise_and(lane, TAPERS - 1) != row
    result = jnp.where(off, value * scale / denominator, 0.0)
    out_ref[0, 0] = result[:, :TAPERS]
    out_ref[0, 1] = result[:, TAPERS : 2 * TAPERS]


def coherence_of(band_edges, parts, total_pixels):
    return pl.pallas_call(
        functools.partial(coherence_kernel, total_pixels),
        out_shape=jax.ShapeDtypeStruct((1, 2, TAPERS, TAPERS), jnp.float32),
        in_specs=[pl.BlockSpec(memory_space=pltpu.SMEM), pl.BlockSpec(memory_space=pltpu.VMEM)],
        name="coherence",
    )(band_edges, parts)


def local(frames, band_edges):
    groups = lax.axis_size("tm")
    n_pix = lax.axis_size("pix")
    frames_dev, pix_dev = frames.shape
    share = pix_dev // groups
    blocks = frames.reshape(frames_dev, groups, share).transpose(1, 0, 2)
    data = lax.all_to_all(blocks, "tm", 0, 0, tiled=True).reshape(NT, share)
    waves = base_waves()
    bin_ids = jnp.arange(NB + 1, dtype=jnp.int32)
    band_of = jnp.sum((bin_ids[:, None] >= band_edges[None, 1:]).astype(jnp.int32), axis=1)
    keep = 1.0 - jnp.any(bin_ids[:, None] == band_edges[None, :], axis=1).astype(jnp.float32)
    sums = band_sums_of(data, waves, band_of, keep, n_pix)
    parts = lax.all_to_all(sums.reshape(groups * n_pix, 1, LANES), ("tm", "pix"), 0, 0, tiled=True)
    return coherence_of(band_edges, parts.reshape(groups * n_pix, LANES), pix_dev * n_pix)


def solution(mesh):
    return jax.shard_map(
        local,
        mesh=mesh,
        in_specs=(P("tm", "pix"), P()),
        out_specs=P("tm", None, None, None),
        check_vma=False,
    )
```

time: 78 us -> 75.1 us (0.963)
  Pallas kernels: 13.1 us -> 9.62 us
  local copies, waits for them, and re-layouts: 3.43 us -> 2.44 us
  other arithmetic: 0.2 us -> 1.1 us
    pallas_call x1, Pallas kernels: 9.69 us -> 7.7 us  [band_sums_of(): pl.pallas_call(spectra_kernel, out_shape=jax.ShapeDtypeStruct((NBANDS, co...]
    pallas_call x1 -> x0, Pallas kernels: 1.49 us -> none  [base_waves(): pl.pallas_call(wave_kernel, out_shape=jax.ShapeDtypeStruct((WAVES, NT), j...]
    unnamed x4 -> x2, local copies, waits for them, and re-layouts: 0.99 us -> 0.01 us
  transfers between devices with their start and end apart: 1 -> 1, of which waited for: 1 -> 1; matrix products, arithmetic and copies ran while one was open for 0% -> 2% of each run, Pallas kernels for 2% -> 0%
where the time goes in v2:
time: 75.1 us; the launch traced here: 74.9 us
  waiting for transfers between devices  26.8 us (36%)
  blocking collectives  21.6 us (29%)
  starting transfers between devices  13.3 us (18%)
  Pallas kernels  9.62 us (13%)
  local copies, waits for them, and re-layouts  2.44 us (3%)
  other arithmetic  1.1 us (1%)
    all_to_all x1, waiting for transfers between devices, local(): data = lax.all_to_all(blocks, 'tm', 0, 0, tiled=True).reshape(NT, share)  26.8 us
    all_to_all x1, blocking collectives, local(): lax.all_to_all(sums.reshape(groups * n_pix, 1, LANES), ('tm', 'pix'), 0,...  21.6 us
    all_to_all x1, starting transfers between devices, local(): data = lax.all_to_all(blocks, 'tm', 0, 0, tiled=True).reshape(NT, share)  13.3 us
    pallas_call x1, Pallas kernels, band_sums_of(): pl.pallas_call(spectra_kernel, out_shape=jax.ShapeDtypeStruct((NBANDS, co...  7.7 us
    reshape x1, local copies, waits for them, and re-layouts, local(): blocks = frames.reshape(frames_dev, groups, share).transpose(1, 0, 2)  2.37 us
    pallas_call x1, Pallas kernels, coherence_of(): pl.pallas_call(functools.partial(coherence_kernel, total_pixels), out_sha...  1.92 us
  transfers between devices with their start and end apart: 1, of which 1 were waited for; matrix products, arithmetic and copies ran while one was open for 2% of the time, Pallas kernels for 0%

profile of v2, /device:TPU:1, one launch (start us, length us, event | category | flops | bytes accessed | tf_op | source)
XLA Modules:
  0.0 74.9 jit_solution(16890277304896635511)
XLA Ops:
  0.0 2.4 %copy.10 = bf16[2,64,8,512]{3,2,0,1:T(8,128)(2,1)} copy(bf16[2,64,8,512]{3,2,1,0:T(8,128)(2,1)} %bitcast.14) | data formatting | bytes 2097152 | tf_op jit(solution)/shard_map/reshape | solution.py:232
  2.4 0.0 copy-start
  2.4 13.3 %all-to-all-start = ((bf16[64,16,512]{2,1,0:T(8,128)(2,1)}), bf16[64,16,512]{2,1,0:T(8,128)(2,1)S(1)}, u32[]{:S(2)}, u32[]{:S(2)}) async-start(bf16[64,16,512]{2,1,0:T(8,128)(2,1)} %bitcast.11), calls=%async_computation | async-start | bytes 2097152 | tf_op jit(solution)/shard_map/all_to_all | solution.py:233
  15.7 0.0 copy-done
  15.7 0.1 slice.3
  15.8 0.1 convert_reduce_fusion.band_ref
  15.9 0.1 fusion
  16.0 0.2 sine_multiply_fusion.taper_ref
  16.2 0.3 fusion.3
  16.4 0.4 fusion.1
  16.9 26.8 %all-to-all-done = bf16[64,16,512]{2,1,0:T(8,128)(2,1)S(1)} async-done(((bf16[64,16,512]{2,1,0:T(8,128)(2,1)}), bf16[64,16,512]{2,1,0:T(8,128)(2,1)S(1)}, u32[]{:S(2)}, u32[]{:S(2)}) %all-to-all-start) | async-done | bytes 1048608 | tf_op jit(solution)/shard_map/all_to_all | solution.py:233
  43.7 7.7 %band_sums.1 = f32[64,4,128]{2,1,0:T(4,128)S(1)} custom-call(s32[385]{0:T(512)S(1)} %convert_reduce_fusion.band_ref, f32[385]{0:T(512)S(1)} %convert_subtract_fusion.keep_ref, f32[16,1024]{1,0:T(8,128)S(1)} %get-tuple-element.8.fine_cos, f32[16,1024]{1,0:T(8,128)S(1)} %get-tuple-element.7.fine_sin, f32[24,1024]{1,0:T(8,128)S(1)} %get-tuple-element.6.coarse_cos, ...), custom_call_target="tpu_custom_call" | custom-call | flops 5905580032 | bytes 2000000 | tf_op jit(solution)/shard_map/band_sums/pallas_call | solution.py:175
  51.4 21.6 %all_to_all.10 = f32[256,1,128]{2,1,0:T(1,128)} all-to-all(f32[256,1,128]{2,1,0:T(1,128)S(1)} %bitcast.13), channel_id=1, replica_groups=mesh['tm'=64,'pix'=4] {'tm','pix'}, dimensions={0} | all-to-all | bytes 262144 | tf_op jit(solution)/shard_map/all_to_all | solution.py:239
  73.0 1.9 %coherence.1 = f32[1,2,8,8]{3,2,1,0:T(8,128)} custom-call(s32[65]{0:T(128)} %edges_ref.1, f32[256,128]{1,0:T(8,128)} %bitcast.15), custom_call_target="tpu_custom_call" | custom-call | tf_op jit(solution)/shard_map/coherence/pallas_call | solution.py:219
  (5 shorter events, 0.0 us)
Async XLA Ops:
  2.4 13.3 %copy-start = (s32[65]{0:T(128)S(1)}, s32[65]{0:T(128)}, u32[]{:S(2)}) copy-start(s32[65]{0:T(128)} %edges_ref.1) | copy-start | bytes 784
  2.4 41.3 %all-to-all-start = ((bf16[64,16,512]{2,1,0:T(8,128)(2,1)}), bf16[64,16,512]{2,1,0:T(8,128)(2,1)S(1)}, u32[]{:S(2)}, u32[]{:S(2)}) async-start(bf16[64,16,512]{2,1,0:T(8,128)(2,1)} %bitcast.11), calls=%async_computation | async-start | bytes 2097152 | tf_op jit(solution)/shard_map/all_to_all | solution.py:233

commit v3 on v2

--- a/solution.py
+++ b/solution.py
@@ -193,6 +193,25 @@
     )(band_of, keep, *waves, data)
 
 
+def split_kernel(frames_ref, blocks_ref, sem):
+    groups, _, share = blocks_ref.shape
+    for j in range(groups):
+        pltpu.make_async_copy(frames_ref.at[:, pl.ds(j * share, share)], blocks_ref.at[j], sem).start()
+    pltpu.make_async_copy(blocks_ref, blocks_ref, sem).wait()
+
+
+def split_pixels(frames, groups):
+    rows, pixels = frames.shape
+    return pl.pallas_call(
+        split_kernel,
+        out_shape=jax.ShapeDtypeStruct((groups, rows, pixels // groups), frames.dtype),
+        in_specs=[pl.BlockSpec(memory_space=pl.ANY)],
+        out_specs=pl.BlockSpec(memory_space=pltpu.VMEM),
+        scratch_shapes=[pltpu.SemaphoreType.DMA],
+        name="split_pixels",
+    )(frames)
+
+
 def coherence_kernel(total_pixels, edges_ref, parts_ref, out_ref):
     own = lax.axis_index("tm")
     count = jnp.full((TAPERS, LANES), edges_ref[own + 1] - edges_ref[own], jnp.int32).astype(jnp.float32)
@@ -227,9 +246,9 @@
 def local(frames, band_edges):
     groups = lax.axis_size("tm")
     n_pix = lax.axis_size("pix")
-    frames_dev, pix_dev = frames.shape
+    pix_dev = frames.shape[1]
     share = pix_dev // groups
-    blocks = frames.reshape(frames_dev, groups, share).transpose(1, 0, 2)
+    blocks = split_pixels(frames, groups)
     data = lax.all_to_all(blocks, "tm", 0, 0, tiled=True).reshape(NT, share)
     waves = base_waves()
     bin_ids = jnp.arange(NB + 1, dtype=jnp.int32)

time: 75.1 us -> 74.9 us (level)
  local copies, waits for them, and re-layouts: 2.44 us -> 0.08 us
  Pallas kernels: 9.62 us -> 11.8 us
    reshape x1 -> x0, local copies, waits for them, and re-layouts: 2.37 us -> none  [local(): blocks = frames.reshape(frames_dev, groups, share).transpose(1, 0, 2)]
    pallas_call x0 -> x1, Pallas kernels: none -> 2.19 us  [split_pixels(): pl.pallas_call(split_kernel, out_shape=jax.ShapeDtypeStruct((groups, rows...]
where the time goes in v3:
time: 74.9 us; the launch traced here: 74.6 us
  waiting for transfers between devices  26.8 us (36%)
  blocking collectives  21.6 us (29%)
  starting transfers between devices  13.2 us (18%)
  Pallas kernels  11.8 us (16%)
  other arithmetic  1.1 us (1%)
    all_to_all x1, waiting for transfers between devices, local(): data = lax.all_to_all(blocks, 'tm', 0, 0, tiled=True).reshape(NT, share)  26.8 us
    all_to_all x1, blocking collectives, local(): lax.all_to_all(sums.reshape(groups * n_pix, 1, LANES), ('tm', 'pix'), 0,...  21.6 us
    all_to_all x1, starting transfers between devices, local(): data = lax.all_to_all(blocks, 'tm', 0, 0, tiled=True).reshape(NT, share)  13.2 us
    pallas_call x1, Pallas kernels, band_sums_of(): pl.pallas_call(spectra_kernel, out_shape=jax.ShapeDtypeStruct((NBANDS, co...  7.72 us
    pallas_call x1, Pallas kernels, split_pixels(): pl.pallas_call(split_kernel, out_shape=jax.ShapeDtypeStruct((groups, rows...  2.19 us
    pallas_call x1, Pallas kernels, coherence_of(): pl.pallas_call(functools.partial(coherence_kernel, total_pixels), out_sha...  1.92 us
  transfers between devices with their start and end apart: 1, of which 1 were waited for; matrix products, arithmetic and copies ran while one was open for 2% of the time, Pallas kernels for 0%

profile of v3, /device:TPU:1, one launch (start us, length us, event | category | flops | bytes accessed | tf_op | source)
XLA Modules:
  0.0 74.6 jit_solution(14945811849299106784)
XLA Ops:
  0.0 2.2 %split_pixels.1 = bf16[64,16,512]{2,1,0:T(8,128)(2,1)} custom-call(bf16[16,32768]{1,0:T(8,128)(2,1)} %frames_ref.1), custom_call_target="tpu_custom_call" | custom-call | tf_op jit(solution)/shard_map/split_pixels/pallas_call | solution.py:205
  2.2 0.0 copy-start
  2.2 13.2 %all-to-all-start = ((bf16[64,16,512]{2,1,0:T(8,128)(2,1)}), bf16[64,16,512]{2,1,0:T(8,128)(2,1)S(1)}, u32[]{:S(2)}, u32[]{:S(2)}) async-start(bf16[64,16,512]{2,1,0:T(8,128)(2,1)} %split_pixels.1), calls=%async_computation | async-start | bytes 2097152 | tf_op jit(solution)/shard_map/all_to_all | solution.py:252
  15.4 0.0 copy-done
  15.4 0.1 slice.3
  15.5 0.1 convert_reduce_fusion.band_ref
  15.6 0.1 fusion
  15.7 0.2 sine_multiply_fusion.taper_ref
  15.9 0.3 fusion.3
  16.2 0.4 fusion.1
  16.6 26.8 %all-to-all-done = bf16[64,16,512]{2,1,0:T(8,128)(2,1)S(1)} async-done(((bf16[64,16,512]{2,1,0:T(8,128)(2,1)}), bf16[64,16,512]{2,1,0:T(8,128)(2,1)S(1)}, u32[]{:S(2)}, u32[]{:S(2)}) %all-to-all-start) | async-done | bytes 1048608 | tf_op jit(solution)/shard_map/all_to_all | solution.py:252
  43.4 7.7 %band_sums.1 = f32[64,4,128]{2,1,0:T(4,128)S(1)} custom-call(s32[385]{0:T(512)S(1)} %convert_reduce_fusion.band_ref, f32[385]{0:T(512)S(1)} %convert_subtract_fusion.keep_ref, f32[16,1024]{1,0:T(8,128)S(1)} %get-tuple-element.8.fine_cos, f32[16,1024]{1,0:T(8,128)S(1)} %get-tuple-element.7.fine_sin, f32[24,1024]{1,0:T(8,128)S(1)} %get-tuple-element.6.coarse_cos, ...), custom_call_target="tpu_custom_call" | custom-call | flops 5905580032 | bytes 2000000 | tf_op jit(solution)/shard_map/band_sums/pallas_call | solution.py:175
  51.1 21.6 %all_to_all.10 = f32[256,1,128]{2,1,0:T(1,128)} all-to-all(f32[256,1,128]{2,1,0:T(1,128)S(1)} %bitcast.6), channel_id=1, replica_groups=mesh['tm'=64,'pix'=4] {'tm','pix'}, dimensions={0} | all-to-all | bytes 262144 | tf_op jit(solution)/shard_map/all_to_all | solution.py:258
  72.7 1.9 %coherence.1 = f32[1,2,8,8]{3,2,1,0:T(8,128)} custom-call(s32[65]{0:T(128)} %edges_ref.1, f32[256,128]{1,0:T(8,128)} %bitcast.7), custom_call_target="tpu_custom_call" | custom-call | tf_op jit(solution)/shard_map/coherence/pallas_call | solution.py:238
  (5 shorter events, 0.0 us)
Async XLA Ops:
  2.2 13.2 %copy-start = (s32[65]{0:T(128)S(1)}, s32[65]{0:T(128)}, u32[]{:S(2)}) copy-start(s32[65]{0:T(128)} %edges_ref.1) | copy-start | bytes 784
  2.2 41.2 %all-to-all-start = ((bf16[64,16,512]{2,1,0:T(8,128)(2,1)}), bf16[64,16,512]{2,1,0:T(8,128)(2,1)S(1)}, u32[]{:S(2)}, u32[]{:S(2)}) async-start(bf16[64,16,512]{2,1,0:T(8,128)(2,1)} %split_pixels.1), calls=%async_computation | async-start | bytes 2097152 | tf_op jit(solution)/shard_map/all_to_all | solution.py:252

commit v4 on v3

--- a/solution.py
+++ b/solution.py
@@ -164,8 +164,9 @@
     for shift in (16, 32, 64):
         value = value + pltpu.roll(value, shift, 2)
     own = (jnp.right_shift(lane, 4) == row)[None]
-    sums = jnp.sum(jnp.where(own, value, 0.0), axis=1, keepdims=True)
-    out_ref[...] = jnp.broadcast_to(sums, out_ref.shape)
+    sums = jnp.sum(jnp.where(own, value, 0.0), axis=1)
+    for i in range(out_ref.shape[0]):
+        out_ref[i] = sums
 
 
 def band_sums_of(data, waves, band_of, keep, copies):
@@ -174,7 +175,7 @@
     macs = NB * TAPERS * NT * pixels * 4 // 3 + STEPS * (2 * ROWS) ** 2 * pixels
     return pl.pallas_call(
         spectra_kernel,
-        out_shape=jax.ShapeDtypeStruct((NBANDS, copies, LANES), jnp.float32),
+        out_shape=jax.ShapeDtypeStruct((copies, NBANDS, LANES), jnp.float32),
         in_specs=[smem, smem] + [vmem] * 6,
         out_specs=vmem,
         scratch_shapes=[
@@ -255,7 +256,7 @@
     band_of = jnp.sum((bin_ids[:, None] >= band_edges[None, 1:]).astype(jnp.int32), axis=1)
     keep = 1.0 - jnp.any(bin_ids[:, None] == band_edges[None, :], axis=1).astype(jnp.float32)
     sums = band_sums_of(data, waves, band_of, keep, n_pix)
-    parts = lax.all_to_all(sums.reshape(groups * n_pix, 1, LANES), ("tm", "pix"), 0, 0, tiled=True)
+    parts = lax.all_to_all(sums.reshape(groups * n_pix, 1, LANES), ("pix", "tm"), 0, 0, tiled=True)
     return coherence_of(band_edges, parts.reshape(groups * n_pix, LANES), pix_dev * n_pix)
 
 

time: 74.9 us -> 75.1 us (level)
  no operation moved by 1% of the time
where the time goes in v4:
time: 75.1 us; the launch traced here: 74.8 us
  waiting for transfers between devices  26.8 us (36%)
  blocking collectives  21.8 us (29%)
  starting transfers between devices  13.2 us (18%)
  Pallas kernels  11.9 us (16%)
  other arithmetic  1.1 us (1%)
    all_to_all x1, waiting for transfers between devices, local(): data = lax.all_to_all(blocks, 'tm', 0, 0, tiled=True).reshape(NT, share)  26.8 us
    all_to_all x1, blocking collectives, local(): lax.all_to_all(sums.reshape(groups * n_pix, 1, LANES), ('pix', 'tm'), 0,...  21.8 us
    all_to_all x1, starting transfers between devices, local(): data = lax.all_to_all(blocks, 'tm', 0, 0, tiled=True).reshape(NT, share)  13.2 us
    pallas_call x1, Pallas kernels, band_sums_of(): pl.pallas_call(spectra_kernel, out_shape=jax.ShapeDtypeStruct((copies, NB...  7.75 us
    pallas_call x1, Pallas kernels, split_pixels(): pl.pallas_call(split_kernel, out_shape=jax.ShapeDtypeStruct((groups, rows...  2.19 us
    pallas_call x1, Pallas kernels, coherence_of(): pl.pallas_call(functools.partial(coherence_kernel, total_pixels), out_sha...  1.92 us
  transfers between devices with their start and end apart: 1, of which 1 were waited for; matrix products, arithmetic and copies ran while one was open for 2% of the time, Pallas kernels for 0%

profile of v4, /device:TPU:1, one launch (start us, length us, event | category | flops | bytes accessed | tf_op | source)
XLA Modules:
  0.0 74.8 jit_solution(15901142126307284464)
XLA Ops:
  0.0 2.2 %split_pixels.1 = bf16[64,16,512]{2,1,0:T(8,128)(2,1)} custom-call(bf16[16,32768]{1,0:T(8,128)(2,1)} %frames_ref.1), custom_call_target="tpu_custom_call" | custom-call | tf_op jit(solution)/shard_map/split_pixels/pallas_call | solution.py:206
  2.2 0.0 copy-start
  2.2 13.2 %all-to-all-start = ((bf16[64,16,512]{2,1,0:T(8,128)(2,1)}), bf16[64,16,512]{2,1,0:T(8,128)(2,1)S(1)}, u32[]{:S(2)}, u32[]{:S(2)}) async-start(bf16[64,16,512]{2,1,0:T(8,128)(2,1)} %split_pixels.1), calls=%async_computation | async-start | bytes 2097152 | tf_op jit(solution)/shard_map/all_to_all | solution.py:253
  15.4 0.0 copy-done
  15.4 0.1 slice.3
  15.5 0.1 convert_reduce_fusion.band_ref
  15.6 0.1 fusion
  15.7 0.2 sine_multiply_fusion.taper_ref
  15.9 0.3 fusion.3
  16.2 0.4 fusion.1
  16.6 26.8 %all-to-all-done = bf16[64,16,512]{2,1,0:T(8,128)(2,1)S(1)} async-done(((bf16[64,16,512]{2,1,0:T(8,128)(2,1)}), bf16[64,16,512]{2,1,0:T(8,128)(2,1)S(1)}, u32[]{:S(2)}, u32[]{:S(2)}) %all-to-all-start) | async-done | bytes 1048608 | tf_op jit(solution)/shard_map/all_to_all | solution.py:253
  43.4 7.7 %band_sums.1 = f32[4,64,128]{2,1,0:T(8,128)S(1)} custom-call(s32[385]{0:T(512)S(1)} %convert_reduce_fusion.band_ref, f32[385]{0:T(512)S(1)} %convert_subtract_fusion.keep_ref, f32[16,1024]{1,0:T(8,128)S(1)} %get-tuple-element.8.fine_cos, f32[16,1024]{1,0:T(8,128)S(1)} %get-tuple-element.7.fine_sin, f32[24,1024]{1,0:T(8,128)S(1)} %get-tuple-element.6.coarse_cos, ...), custom_call_target="tpu_custom_call" | custom-call | flops 5905580032 | bytes 2000000 | tf_op jit(solution)/shard_map/band_sums/pallas_call | solution.py:176
  51.1 21.8 %all_to_all.10 = f32[256,1,128]{2,1,0:T(1,128)} all-to-all(f32[256,1,128]{2,1,0:T(1,128)S(1)} %bitcast.6), channel_id=1, replica_groups=mesh['tm'=64,'pix'=4] {'pix','tm'}, dimensions={0} | all-to-all | bytes 262144 | tf_op jit(solution)/shard_map/all_to_all | solution.py:259
  72.9 1.9 %coherence.1 = f32[1,2,8,8]{3,2,1,0:T(8,128)} custom-call(s32[65]{0:T(128)} %edges_ref.1, f32[256,128]{1,0:T(8,128)} %bitcast.7), custom_call_target="tpu_custom_call" | custom-call | tf_op jit(solution)/shard_map/coherence/pallas_call | solution.py:239
  (5 shorter events, 0.0 us)
Async XLA Ops:
  2.2 13.2 %copy-start = (s32[65]{0:T(128)S(1)}, s32[65]{0:T(128)}, u32[]{:S(2)}) copy-start(s32[65]{0:T(128)} %edges_ref.1) | copy-start | bytes 784
  2.2 41.2 %all-to-all-start = ((bf16[64,16,512]{2,1,0:T(8,128)(2,1)}), bf16[64,16,512]{2,1,0:T(8,128)(2,1)S(1)}, u32[]{:S(2)}, u32[]{:S(2)}) async-start(bf16[64,16,512]{2,1,0:T(8,128)(2,1)} %split_pixels.1), calls=%async_computation | async-start | bytes 2097152 | tf_op jit(solution)/shard_map/all_to_all | solution.py:253
